TPU v7x, 256 devices: a whole 4x4x8 slice. The times are simulated.
256 devices in a mesh: section: 16 (over z_lo, x, core), expert: 16 (over z_hi, y).
Axes of the slice: x: 4, y: 4, z: 8 (z_hi: 4, z_lo: 2; z = z_hi * 2 + z_lo), core: 2. Of those that a mesh axis runs over, the one named last changes fastest.
Arguments:
- hidden: bfloat16 [16, 16, 1024, 1024], P('section', 'expert'), may hold values from -6 to 6
- down_weight: bfloat16 [16, 16, 1024, 3584], P('section', 'expert'), may hold values from -0.1875 to 0.1875
- expert_ids: int32 [65536, 2], P(('section', 'expert')), may hold values from 0 to 15, all different within a row; in each aligned block of 256 rows (0 to 255, 256 to 511, ...) at most 64 rows name the same one
- route_gates: bfloat16 [65536, 2], P(('section', 'expert')), may hold values from 0.099609375 to 1
- residual: bfloat16 [65536, 3584], P(('section', 'expert')), may hold values from -6 to 6
Outputs:
- handoff: bfloat16 [65536, 3584], P(('section', 'expert'))
Inputs may be any that keep to these rules, and one draw needn't show every extreme that they name: `expert_ids`: each row names 2 different experts; in the rows of one device no expert is named by more than 64 rows, a bound that some block reaches.
All inputs are finite; a program needn't handle non-finite values.
Results may differ from a plain program's by a relative error of at most 0.0048.
Values may be sent and summed in bfloat16 or wider, within the bound.
A program may use at most 128 MiB of HBM per device.

v0:
```python
import jax
import jax.numpy as jnp
from jax import lax
from jax.sharding import PartitionSpec as P


def shifted(value, axis, steps):
    count = lax.axis_size(axis)
    pairs = [(source, (source + steps) % count) for source in range(count)]
    return lax.ppermute(value, axis, pairs)


def slot_table(route_ids, route_gates, experts, capacity):
    rows_here, routes = route_ids.shape
    flat_ids = route_ids.reshape(-1)
    expert_cols = jnp.arange(experts, dtype=jnp.int32)
    onehot = (flat_ids[:, None] == expert_cols[None, :]).astype(jnp.int32)
    before = jnp.cumsum(onehot, axis=0) - onehot
    position = jnp.sum(before * onehot, axis=1)
    target = flat_ids * capacity + position
    columns = jnp.arange(experts * capacity, dtype=jnp.int32)
    matched = target[:, None] == columns[None, :]
    weighted = jnp.where(matched, route_gates.reshape(-1)[:, None].astype(jnp.float32), 0.0)
    weighted = jnp.sum(weighted.reshape(rows_here, routes, experts * capacity), axis=1)
    return weighted.astype(jnp.bfloat16)


def combine(produced, mixing_table):
    column_block = lax.all_to_all(produced, "expert", split_axis=0, concat_axis=0, tiled=True)
    flat_block = column_block.reshape(-1, column_block.shape[2])
    summed = jnp.dot(mixing_table, flat_block, preferred_element_type=jnp.float32)
    return lax.optimization_barrier(summed.astype(jnp.bfloat16))


def local(hidden, down_weight, expert_ids, route_gates, residual):
    experts = lax.axis_size("expert")
    capacity = hidden.shape[2] // experts
    produced = jnp.dot(hidden[0, 0], down_weight[0, 0], preferred_element_type=jnp.float32)
    produced = produced.astype(jnp.bfloat16).reshape(experts, capacity, produced.shape[1])
    mixing_table = slot_table(expert_ids, route_gates, experts, capacity)
    branch = combine(produced, mixing_table)
    layer_out = (residual.astype(jnp.float32) + branch.astype(jnp.float32)).astype(jnp.bfloat16)
    return shifted(layer_out, "section", 1)


def solution(mesh):
    return jax.shard_map(
        local,
        mesh=mesh,
        in_specs=(
            P("section", "expert", None, None),
            P("section", "expert", None, None),
            P(("section", "expert"), None),
            P(("section", "expert"), None),
            P(("section", "expert"), None),
        ),
        out_specs=P(("section", "expert"), None),
        check_vma=False,
    )
```

profile of v0, /device:TPU:32, one launch (start us, length us, event | category | flops | bytes accessed | tf_op | source)
XLA Modules:
  0.0 223.6 jit_solution(12137455864851073677)
XLA Ops:
  0.0 0.0 copy-start
  0.0 1.6 copy-done
  1.6 12.7 %convolution_convert_fusion = bf16[1024,3584]{1,0:T(8,128)(2,1)} fusion(bf16[1,1,1024,3584]{3,2,1,0:T(8,128)(2,1)} %param.6, bf16[1,1,1024,1024]{3,2,1,0:T(8,128)(2,1)S(1)} %copy-done), kind=kOutput, calls=%fused_computation | convolution fusion | flops 7519862784 | bytes 16777216 | tf_op jit(solution)/shard_map/dot_general | solution.py:38
  14.3 0.0 copy-start.2
  14.3 0.0 copy-start.3
  14.3 10.5 %all-to-all-start = ((bf16[16,64,3584]{2,1,0:T(8,128)(2,1)}), bf16[16,64,3584]{2,1,0:T(8,128)(2,1)}, u32[]{:S(2)}, u32[]{:S(2)}) async-start(bf16[16,64,3584]{2,1,0:T(8,128)(2,1)} %bitcast.29), calls=%async_computation | async-start | bytes 14680064 | tf_op jit(solution)/shard_map/all_to_all | solution.py:29
  24.8 0.0 copy-done.2
  24.8 0.1 copy.20
  25.0 0.1 eq.39
  25.1 0.1 eq.43
  25.3 0.0 copy-done.3
  25.3 1.2 reduce-window.6
  26.4 0.2 slice_reduce_fusion
  26.7 0.1 fusion.5
  26.8 0.1 reduce_sum.21
  27.0 0.1 copy.23
  27.0 0.3 select_reduce_fusion
  27.3 164.4 %all-to-all-done = bf16[16,64,3584]{2,1,0:T(8,128)(2,1)} async-done(((bf16[16,64,3584]{2,1,0:T(8,128)(2,1)}), bf16[16,64,3584]{2,1,0:T(8,128)(2,1)}, u32[]{:S(2)}, u32[]{:S(2)}) %all-to-all-start) | async-done | bytes 7340064 | tf_op jit(solution)/shard_map/all_to_all | solution.py:29
  191.8 0.0 copy-start.1
  191.8 5.3 %convolution_convert_fusion.1 = bf16[256,3584]{1,0:T(8,128)(2,1)S(1)} fusion(bf16[1024,3584]{1,0:T(8,128)(2,1)} %bitcast.4, bf16[256,1024]{1,0:T(8,128)(2,1)S(1)} %select_reduce_fusion), kind=kOutput, calls=%fused_computation.2 | convolution fusion | flops 1879965696 | bytes 9699328 | tf_op jit(solution)/shard_map/dot_general | solution.py:31
  197.0 0.0 copy-done.1
  197.1 0.4 add_convert_fusion
  197.5 0.1 collective-permute-start
  197.6 24.7 %collective-permute-done = bf16[256,3584]{1,0:T(8,128)(2,1)S(1)} collective-permute-done((bf16[256,3584]{1,0:T(8,128)(2,1)S(1)}, bf16[256,3584]{1,0:T(8,128)(2,1)S(1)}, u32[]{:S(2)}, u32[]{:S(2)}) %collective-permute-start) | collective-permute-done | bytes 1835040 | tf_op jit(solution)/shard_map/ppermute | solution.py:10
  222.3 1.2 copy.27
  (5 shorter events, 0.1 us)
Async XLA Ops:
  0.0 1.6 copy-start
  14.3 10.5 %copy-start.2 = (s32[256,2]{0,1:T(2,128)S(1)}, s32[256,2]{0,1:T(2,128)}, u32[]{:S(2)}) copy-start(s32[256,2]{0,1:T(2,128)} %param.7) | copy-start | bytes 6148
  14.3 10.9 %copy-start.3 = (bf16[256,2]{0,1:T(2,128)(2,1)S(1)}, bf16[256,2]{0,1:T(2,128)(2,1)}, u32[]{:S(2)}) copy-start(bf16[256,2]{0,1:T(2,128)(2,1)} %param.8) | copy-start | bytes 3076
  14.3 177.4 %all-to-all-start = ((bf16[16,64,3584]{2,1,0:T(8,128)(2,1)}), bf16[16,64,3584]{2,1,0:T(8,128)(2,1)}, u32[]{:S(2)}, u32[]{:S(2)}) async-start(bf16[16,64,3584]{2,1,0:T(8,128)(2,1)} %bitcast.29), calls=%async_computation | async-start | bytes 14680064 | tf_op jit(solution)/shard_map/all_to_all | solution.py:29
  191.8 5.3 %copy-start.1 = (bf16[256,3584]{1,0:T(8,128)(2,1)S(1)}, bf16[256,3584]{1,0:T(8,128)(2,1)}, u32[]{:S(2)}) copy-start(bf16[256,3584]{1,0:T(8,128)(2,1)} %param.9) | copy-start | bytes 5505028
  197.5 24.8 %collective-permute-start = (bf16[256,3584]{1,0:T(8,128)(2,1)S(1)}, bf16[256,3584]{1,0:T(8,128)(2,1)S(1)}, u32[]{:S(2)}, u32[]{:S(2)}) collective-permute-start(bf16[256,3584]{1,0:T(8,128)(2,1)S(1)} %add_convert_fusion), channel_id=1, source_target_pairs={{0,16},{16,32},{32,48},{48,64},{64,80},{80,96},{96,112},{112,128},... | collective-permute-start | bytes 5505032 | tf_op jit(solution)/shard_map/ppermute | solution.py:10
where the time goes:
time: 224 us
  waiting for transfers between devices  189 us (84%)
  matrix products  18 us (8%)
  starting transfers between devices  10.6 us (5%)
  local copies, waits for them, and re-layouts  3.69 us (2%)
    all_to_all x1, waiting for transfers between devices, combine(): lax.all_to_all(produced, 'expert', split_axis=0, concat_axis=0, tiled=True)  164 us
    ppermute x1, waiting for transfers between devices, shifted(): return lax.ppermute(value, axis, pairs)  24.7 us
    dot_general x1, matrix products, local(): jnp.dot(hidden[0, 0], down_weight[0, 0], preferred_element_type=jnp.float32)  12.7 us
    all_to_all x1, starting transfers between devices, combine(): lax.all_to_all(produced, 'expert', split_axis=0, concat_axis=0, tiled=True)  10.5 us
    dot_general x1, matrix products, combine(): jnp.dot(mixing_table, flat_block, preferred_element_type=jnp.float32)  5.27 us
  transfers between devices with their start and end apart: 2, of which 2 were waited for; matrix products, arithmetic and copies ran while one was open for 1% of the time, Pallas kernels for 0%

commit v1 on v0

v1 whole, which is shorter than its diff:
```python
import functools

import jax
import jax.numpy as jnp
from jax import lax
from jax.experimental import pallas as pl
from jax.experimental.pallas import tpu as pltpu
from jax.sharding import PartitionSpec as P

MESH = pl.DeviceIdType.MESH
SIDE = 4
CHUNK = 256
HALF = CHUNK // 2
UP, DOWN = 0, 1


def kernel(
    sections, chunks, cap,
    hidden_hbm, weight_hbm, ids_ref, gates_ref, residual_hbm,
    out_hbm,
    hidden, weight, residual, ysend, yrecv, far_send, far_recv, near_send, near_recv, layer,
    table, mixing,
    hidden_sem, weight_sem, residual_sem, table_send, table_recv,
    y_ssem, y_rsem, far_ssem, far_rsem, near_ssem, near_rsem, hand_ssem, hand_rsem,
):
    s, e = lax.axis_index("section"), lax.axis_index("expert")
    z, y = e // SIDE, e % SIDE
    group = SIDE * cap
    rows = ids_ref.shape[1]

    def at_y(step):
        return (s, z * SIDE + (y + step) % SIDE)

    def at_z(step):
        return (s, ((z + step) % SIDE) * SIDE + y)

    following = ((s + 1) % sections, e)
    preceding = ((s + sections - 1) % sections, e)

    barrier = pltpu.get_barrier_semaphore()
    partners = [at_y(1), at_y(2), at_y(3), at_z(1), at_z(2), at_z(3), preceding]
    for partner in partners:
        pl.semaphore_signal(barrier, inc=1, device_id=partner, device_id_type=MESH)

    def columns(c):
        return pl.ds(pl.multiple_of(c * CHUNK, CHUNK), CHUNK)

    def load_weight(c):
        return pltpu.make_async_copy(weight_hbm.at[0, 0, :, columns(c)], weight.at[c], weight_sem.at[c])

    def load_residual(c):
        return pltpu.make_async_copy(residual_hbm.at[:, columns(c)], residual.at[c], residual_sem.at[c])

    load_hidden = pltpu.make_async_copy(hidden_hbm.at[0, 0], hidden, hidden_sem)
    load_hidden.start()

    @pl.loop(0, chunks)
    def _(c):
        load_weight(c).start()

    @pl.loop(0, chunks)
    def _(c):
        load_residual(c).start()

    ids = ids_ref[...]
    experts = lax.broadcasted_iota(jnp.int32, (SIDE * SIDE, rows), 0)
    named = [(experts == ids[k:k + 1]).astype(jnp.float32) for k in range(2)]
    earlier = (lax.broadcasted_iota(jnp.int32, (rows, rows), 0) < lax.broadcasted_iota(jnp.int32, (rows, rows), 1))
    before = jnp.dot(
        (named[0] + named[1]).astype(jnp.bfloat16), earlier.astype(jnp.bfloat16), preferred_element_type=jnp.float32
    )
    slots = [
        ids[k:k + 1].astype(jnp.float32) * cap + jnp.sum(before * named[k], axis=0, keepdims=True) for k in range(2)
    ]
    gates = gates_ref[...].astype(jnp.float32)
    table[z] = jnp.concatenate([slots[0], slots[1], gates, jnp.zeros((4, rows), jnp.float32)], axis=0)

    def produce(c):
        load_weight(c).wait()
        for zd in range(SIDE):
            block = jnp.dot(
                hidden[zd * group:(zd + 1) * group], weight[c], preferred_element_type=jnp.float32
            ).astype(jnp.bfloat16)
            ysend[c, :, zd] = block.reshape(SIDE, cap, CHUNK)
        yrecv[c, :, y] = ysend[c, y]

    def y_copy(c, step):
        yd = (y + step) % SIDE
        return pltpu.make_async_remote_copy(
            src_ref=ysend.at[c, yd], dst_ref=yrecv.at[c, :, y],
            send_sem=y_ssem.at[c, step - 1], recv_sem=y_rsem.at[c, step - 1],
            device_id=at_y(step), device_id_type=MESH,
        )

    def table_copy(step):
        return pltpu.make_async_remote_copy(
            src_ref=table.at[z], dst_ref=table.at[z],
            send_sem=table_send.at[step - 1], recv_sem=table_recv.at[step - 1],
            device_id=at_z(step), device_id_type=MESH,
        )

    def far_copy(c, way):
        return pltpu.make_async_remote_copy(
            src_ref=far_send.at[c, way], dst_ref=far_recv.at[c, way],
            send_sem=far_ssem.at[c, way], recv_sem=far_rsem.at[c, way],
            device_id=at_z(1 if way == UP else 3), device_id_type=MESH,
        )

    def near_copy(c, way, part):
        return pltpu.make_async_remote_copy(
            src_ref=near_send.at[c, way, part], dst_ref=near_recv.at[c, way, part],
            send_sem=near_ssem.at[c, way, part], recv_sem=near_rsem.at[c, way, part],
            device_id=at_z(1 if way == UP else 3), device_id_type=MESH,
        )

    def hand_copy(c):
        return pltpu.make_async_remote_copy(
            src_ref=layer.at[c], dst_ref=out_hbm.at[:, columns(c)],
            send_sem=hand_ssem.at[c], recv_sem=hand_rsem.at[c],
            device_id=following, device_id_type=MESH,
        )

    def partial(c, step, part):
        zd = (z + step) % SIDE
        mine = yrecv[c, zd].reshape(group, CHUNK)
        if part is not None:
            mine = mine[:, part * HALF:(part + 1) * HALF]
        return jnp.dot(mixing[zd], mine, preferred_element_type=jnp.float32)

    def scatter(c):
        for step in (1, 2, 3):
            y_copy(c, step).wait_recv()
        for way in (UP, DOWN):
            far_send[c, way] = partial(c, 2, 1 - way).astype(jnp.bfloat16)
            far_copy(c, way).start()
        for way in (UP, DOWN):
            near_send[c, way, way] = partial(c, 1 if way == UP else 3, way).astype(jnp.bfloat16)
            near_copy(c, way, way).start()

    def pass_on(c):
        for way in (UP, DOWN):
            own = partial(c, 1 if way == UP else 3, 1 - way)
            far_copy(c, way).wait_recv()
            near_send[c, way, 1 - way] = (own + far_recv[c, way].astype(jnp.float32)).astype(jnp.bfloat16)
            near_copy(c, way, 1 - way).start()

    def finish(c):
        own = partial(c, 0, None)
        for way in (UP, DOWN):
            for part in (0, 1):
                near_copy(c, way, part).wait_recv()
        load_residual(c).wait()
        for part in (0, 1):
            cols = slice(part * HALF, (part + 1) * HALF)
            branch = own[:, cols] + near_recv[c, UP, part].astype(jnp.float32) + near_recv[c, DOWN, part].astype(jnp.float32)
            branch = branch.astype(jnp.bfloat16).astype(jnp.float32)
            layer[c, :, cols] = (residual[c, :, cols].astype(jnp.float32) + branch).astype(jnp.bfloat16)
        hand_copy(c).start()

    def mix():
        for step in (1, 2, 3):
            table_copy(step).wait_recv()
        slot = lax.broadcasted_iota(jnp.int32, (group, rows), 0).astype(jnp.float32) + (z * group).astype(jnp.float32)
        for zd in range(SIDE):
            entry = table[zd]
            weights = jnp.where(slot == entry[0:1], entry[2:3], 0.0) + jnp.where(slot == entry[1:2], entry[3:4], 0.0)
            mixing[zd] = weights.T.astype(jnp.bfloat16)

    load_hidden.wait()
    produce(0)
    pl.semaphore_wait(barrier, len(partners))
    for step in (1, 2, 3):
        y_copy(0, step).start()
    for step in (1, 2, 3):
        table_copy(step).start()

    @pl.loop(0, chunks + 2)
    def _(i):
        @pl.when(i < chunks - 1)
        def _():
            produce(i + 1)
            for step in (1, 2, 3):
                y_copy(i + 1, step).start()

        @pl.when(i == 0)
        def _():
            mix()

        @pl.when(i < chunks)
        def _():
            scatter(i)

        @pl.when((i >= 1) & (i <= chunks))
        def _():
            pass_on(i - 1)

        @pl.when(i >= 2)
        def _():
            finish(i - 2)

    @pl.loop(0, chunks)
    def _(c):
        for step in (1, 2, 3):
            y_copy(c, step).wait_send()
        for way in (UP, DOWN):
            far_copy(c, way).wait_send()
            for part in (0, 1):
                near_copy(c, way, part).wait_send()
        hand_copy(c).wait()

    for step in (1, 2, 3):
        table_copy(step).wait_send()


def local(hidden, down_weight, expert_ids, route_gates, residual):
    sections = lax.axis_size("section")
    slots, depth = hidden.shape[2:]
    rows, width = residual.shape
    cap = slots // (SIDE * SIDE)
    chunks = width // CHUNK
    group = SIDE * cap
    bf16, f32 = jnp.bfloat16, jnp.float32
    anywhere = pl.BlockSpec(memory_space=pl.ANY)
    vmem = pl.BlockSpec(memory_space=pltpu.VMEM)
    dma = pltpu.SemaphoreType.DMA
    return pl.pallas_call(
        functools.partial(kernel, sections, chunks, cap),
        out_shape=jax.ShapeDtypeStruct((rows, width), bf16),
        in_specs=[anywhere, anywhere, vmem, vmem, anywhere],
        out_specs=anywhere,
        scratch_shapes=[
            pltpu.VMEM((slots, depth), bf16),
            pltpu.VMEM((chunks, depth, CHUNK), bf16),
            pltpu.VMEM((chunks, rows, CHUNK), bf16),
            pltpu.VMEM((chunks, SIDE, SIDE, cap, CHUNK), bf16),
            pltpu.VMEM((chunks, SIDE, SIDE, cap, CHUNK), bf16),
            pltpu.VMEM((chunks, 2, rows, HALF), bf16),
            pltpu.VMEM((chunks, 2, rows, HALF), bf16),
            pltpu.VMEM((chunks, 2, 2, rows, HALF), bf16),
            pltpu.VMEM((chunks, 2, 2, rows, HALF), bf16),
            pltpu.VMEM((chunks, rows, CHUNK), bf16),
            pltpu.VMEM((SIDE, 8, rows), f32),
            pltpu.VMEM((SIDE, rows, group), bf16),
            dma(()), dma((chunks,)), dma((chunks,)), dma((3,)), dma((3,)),
            dma((chunks, 3)), dma((chunks, 3)),
            dma((chunks, 2)), dma((chunks, 2)),
            dma((chunks, 2, 2)), dma((chunks, 2, 2)),
            dma((chunks,)), dma((chunks,)),
        ],
        compiler_params=pltpu.CompilerParams(
            collective_id=0, has_side_effects=True, vmem_limit_bytes=56 * 2**20
        ),
        cost_estimate=pl.CostEstimate(
            flops=2 * slots * width * (depth + rows), bytes_accessed=2 * (slots * depth + depth * width + 2 * rows * width),
            transcendentals=0,
        ),
        name="down_combine_handoff",
    )(hidden, down_weight, expert_ids.T, route_gates.T, residual)


def solution(mesh):
    return jax.shard_map(
        local,
        mesh=mesh,
        in_specs=(
            P("section", "expert", None, None),
            P("section", "expert", None, None),
            P(("section", "expert"), None),
            P(("section", "expert"), None),
            P(("section", "expert"), None),
        ),
        out_specs=P(("section", "expert"), None),
        check_vma=False,
    )
```

time: 224 us -> 165 us (0.74)
  waiting for transfers between devices: 189 us -> 0 us
  Pallas kernels: 0 us -> 162 us
  matrix products: 18 us -> 0 us
  starting transfers between devices: 10.6 us -> 0 us
    all_to_all x1 -> x0, waiting for transfers between devices: 164 us -> none  [combine(): lax.all_to_all(produced, 'expert', split_axis=0, concat_axis=0, tiled=True)]
    pallas_call x0 -> x1, Pallas kernels: none -> 162 us  [local(): pl.pallas_call(functools.partial(kernel, sections, chunks, cap), out_shap...]
    ppermute x1 -> x0, waiting for transfers between devices: 24.7 us -> none  [shifted(): return lax.ppermute(value, axis, pairs)]
    dot_general x2 -> x0, matrix products: 18 us -> none  [the longest x1 12.7 us: local(): jnp.dot(hidden[0, 0], down_weight[0, 0], preferred_element_type=jnp.float32)]
    all_to_all x1 -> x0, starting transfers between devices: 10.5 us -> none  [combine(): lax.all_to_all(produced, 'expert', split_axis=0, concat_axis=0, tiled=True)]
  transfers between devices with their start and end apart: 2 -> 0, of which waited for: 2 -> 0; matrix products, arithmetic and copies ran while one was open for 1% -> 0% of each run, Pallas kernels for 0% -> 0%
where the time goes in v1:
time: 165 us
  Pallas kernels  162 us (98%)
  local copies, waits for them, and re-layouts  2.85 us (2%)
    pallas_call x1, Pallas kernels, local(): pl.pallas_call(functools.partial(kernel, sections, chunks, cap), out_shap...  162 us

profile of v1, /device:TPU:32, one launch (start us, length us, event | category | flops | bytes accessed | tf_op | source)
XLA Modules:
  0.0 165.1 jit_solution(16283787679851872273)
XLA Ops:
  0.0 162.2 %down_combine_handoff.1 = bf16[256,3584]{1,0:T(8,128)(2,1)} custom-call(bf16[1,1,1024,1024]{3,2,1,0:T(8,128)(2,1)} %hidden_hbm.1, bf16[1,1,1024,3584]{3,2,1,0:T(8,128)(2,1)} %weight_hbm.1, s32[2,256]{1,0:T(2,128)} %bitcast.2, bf16[2,256]{1,0:T(2,128)(2,1)} %bitcast.3, bf16[256,3584]{1,0:T(8,128)(2,1)} %residual_hbm.1), custom_call_target="tpu_custom_call" | custom-call | flops 9395240960 | bytes 13107200 | tf_op jit(solution)/shard_map/down_combine_handoff/pallas_call | solution.py:226
  162.2 2.8 %copy.7 = bf16[256,3584]{1,0:T(8,128)(2,1)} copy(bf16[256,3584]{1,0:T(8,128)(2,1)} %down_combine_handoff.1) | data formatting | bytes 3670016

commit v2 on v1

v2 whole, which is shorter than its diff:
```python
import functools

import jax
import jax.numpy as jnp
from jax import lax
from jax.experimental import pallas as pl
from jax.experimental.pallas import tpu as pltpu
from jax.sharding import PartitionSpec as P

MESH = pl.DeviceIdType.MESH
SIDE = 4
RUN = 8
CHUNK = 256
IN_VMEM = True
READ = 4
AHEAD = 1
STEPS = (2, 1, 3, 0)
FAR, NEAR, OWN = slice(0, 1), slice(1, 3), slice(3, 4)
ALL = slice(0, 4)
UP, DOWN = 0, 1


def kernel(
    sections, chunks, cap,
    hidden_hbm, weight_hbm, ids_ref, gates_ref, residual_hbm,
    out_hbm,
    hidden, weight, residual, ysend, yrecv, far_send, far_recv, near_send, near_recv, twin_send, twin_recv, layer,
    table, mixing,
    hidden_sem, weight_sem, residual_sem, table_send, table_recv,
    y_ssem, y_rsem, far_ssem, far_rsem, near_ssem, near_rsem, twin_ssem, twin_rsem, hand_ssem, hand_rsem,
):
    s, e = lax.axis_index("section"), lax.axis_index("expert")
    z, y = e // SIDE, e % SIDE
    group = SIDE * cap
    rows = ids_ref.shape[1]
    half = rows // 2

    def at_y(step):
        return (s, z * SIDE + (y + step) % SIDE)

    def at_z(step, section=s):
        return (section, ((z + step) % SIDE) * SIDE + y)

    last = s % RUN == RUN - 1
    twin = (s + RUN) % sections
    lent = jnp.where(s < RUN, DOWN, UP)
    following = (jnp.where(last, (twin + 1) % sections, (s + 1) % sections), e)
    preceding = (jnp.where(s % RUN == 0, (s + RUN - 1) % sections, (s + sections - 1) % sections), e)
    lender = at_z(jnp.where(s < RUN, SIDE - 1, 1), twin)

    barrier = pltpu.get_barrier_semaphore()
    partners = [at_y(1), at_y(2), at_y(3), at_z(1), at_z(2), at_z(3), preceding]
    for partner in partners:
        pl.semaphore_signal(barrier, inc=1, device_id=partner, device_id_type=MESH)

    @pl.when(last)
    def _():
        for partner in (lender, (twin, e)):
            pl.semaphore_signal(barrier, inc=1, device_id=partner, device_id_type=MESH)

    def columns(c):
        return pl.ds(pl.multiple_of(c * CHUNK, CHUNK), CHUNK)

    def load_weight(c):
        return pltpu.make_async_copy(weight_hbm.at[0, 0, :, columns(c)], weight.at[c], weight_sem.at[c])

    def load_residual(c):
        return pltpu.make_async_copy(residual_hbm.at[:, columns(c)], residual.at[c], residual_sem.at[c])

    def load_hidden(place):
        block = pl.ds(pl.multiple_of(((z + STEPS[place]) % SIDE) * group, group), group)
        return pltpu.make_async_copy(hidden_hbm.at[0, 0, block], hidden.at[place], hidden_sem.at[place])

    load_hidden(0).start()
    load_weight(0).start()
    for place in (1, 2, 3):
        load_hidden(place).start()

    ids = ids_ref[...]
    experts = lax.broadcasted_iota(jnp.int32, (SIDE * SIDE, rows), 0)
    named = [(experts == ids[k:k + 1]).astype(jnp.float32) for k in range(2)]
    earlier = (lax.broadcasted_iota(jnp.int32, (rows, rows), 0) < lax.broadcasted_iota(jnp.int32, (rows, rows), 1))
    before = jnp.dot(
        (named[0] + named[1]).astype(jnp.bfloat16), earlier.astype(jnp.bfloat16), preferred_element_type=jnp.float32
    )
    slots = [
        ids[k:k + 1].astype(jnp.float32) * cap + jnp.sum(before * named[k], axis=0, keepdims=True) for k in range(2)
    ]
    gates = gates_ref[...].astype(jnp.float32)
    table[z] = jnp.concatenate([slots[0], slots[1], gates, jnp.zeros((4, rows), jnp.float32)], axis=0)

    def produce_block(c, place):
        block = jnp.dot(hidden[place], weight[c], preferred_element_type=jnp.float32).astype(jnp.bfloat16)
        ysend[c, :, place] = block.reshape(SIDE, cap, CHUNK)
        yrecv[c, place, y] = ysend[c, y, place]

    def produce(c):
        load_weight(c).wait()
        for place in range(SIDE):
            produce_block(c, place)

    def y_copy(c, step, part):
        yd = (y + step) % SIDE
        number = (FAR, NEAR, OWN, ALL).index(part) % 3
        return pltpu.make_async_remote_copy(
            src_ref=ysend.at[c, yd, part], dst_ref=yrecv.at[c, part, y],
            send_sem=y_ssem.at[c, step - 1, number], recv_sem=y_rsem.at[c, step - 1, number],
            device_id=at_y(step), device_id_type=MESH,
        )

    def y_start(c, *parts):
        for part in parts:
            for step in (1, 2, 3):
                y_copy(c, step, part).start()

    def y_wait(c, part):
        for step in (1, 2, 3):
            y_copy(c, step, part).wait_recv()

    def table_copy(step):
        return pltpu.make_async_remote_copy(
            src_ref=table.at[z], dst_ref=table.at[z],
            send_sem=table_send.at[step - 1], recv_sem=table_recv.at[step - 1],
            device_id=at_z(step), device_id_type=MESH,
        )

    def far_copy(c, way):
        return pltpu.make_async_remote_copy(
            src_ref=far_send.at[c, way], dst_ref=far_recv.at[c, way],
            send_sem=far_ssem.at[c, way], recv_sem=far_rsem.at[c, way],
            device_id=at_z(1 if way == UP else 3), device_id_type=MESH,
        )

    def near_copy(c, way, part):
        lend = last & (lent == way)
        slot = jnp.where(lend, 1 - way, way)
        return pltpu.make_async_remote_copy(
            src_ref=near_send.at[c, way, part], dst_ref=near_recv.at[c, slot, part],
            send_sem=near_ssem.at[c, way, part], recv_sem=near_rsem.at[c, slot, part],
            device_id=at_z(1 if way == UP else 3, jnp.where(lend, twin, s)), device_id_type=MESH,
        )

    def near_wait(c, way):
        for part in (0, 1):
            pltpu.make_async_remote_copy(
                src_ref=near_send.at[c, way, part], dst_ref=near_recv.at[c, way, part],
                send_sem=near_ssem.at[c, way, part], recv_sem=near_rsem.at[c, way, part],
                device_id=at_z(1), device_id_type=MESH,
            ).wait_recv()

    def twin_copy(c):
        return pltpu.make_async_remote_copy(
            src_ref=twin_send.at[c], dst_ref=twin_recv.at[c],
            send_sem=twin_ssem.at[c], recv_sem=twin_rsem.at[c],
            device_id=(twin, e), device_id_type=MESH,
        )

    def hand_copy(c):
        return pltpu.make_async_remote_copy(
            src_ref=layer.at[c], dst_ref=out_hbm.at[:, columns(c)],
            send_sem=hand_ssem.at[c], recv_sem=hand_rsem.at[c],
            device_id=following, device_id_type=MESH,
        )

    def part_rows(part):
        return slice(part * half, (part + 1) * half)

    def partial(c, step, part):
        place = STEPS.index(step)
        mine = yrecv[c, place].reshape(group, CHUNK)
        return jnp.dot(mixing[place, part_rows(part)], mine, preferred_element_type=jnp.float32)

    def send_far(c):
        for way in (UP, DOWN):
            far_send[c, way] = partial(c, 2, 1 - way).astype(jnp.bfloat16)
            far_copy(c, way).start()

    def send_near(c):
        for way in (UP, DOWN):
            near_send[c, way, way] = partial(c, 1 if way == UP else 3, way).astype(jnp.bfloat16)
            near_copy(c, way, way).start()

    def pass_on(c):
        for way in (UP, DOWN):
            own = partial(c, 1 if way == UP else 3, 1 - way)
            far_copy(c, way).wait_recv()
            near_send[c, way, 1 - way] = (own + far_recv[c, way].astype(jnp.float32)).astype(jnp.bfloat16)
            near_copy(c, way, 1 - way).start()

    def finish(c):
        load_residual(c).wait()

        @pl.when(jnp.logical_not(last))
        def _():
            own = [partial(c, 0, part) for part in (0, 1)]
            near_wait(c, UP)
            near_wait(c, DOWN)
            for part in (0, 1):
                branch = own[part] + near_recv[c, UP, part].astype(jnp.float32) + near_recv[c, DOWN, part].astype(jnp.float32)
                branch = branch.astype(jnp.bfloat16).astype(jnp.float32)
                kept = residual[c, part_rows(part)].astype(jnp.float32)
                layer[c, part_rows(part)] = (kept + branch).astype(jnp.bfloat16)
            hand_copy(c).start()

        for way, here in ((UP, s < RUN), (DOWN, s >= RUN)):
            @pl.when(last & here)
            def _():
                own = [partial(c, 0, part) for part in (0, 1)]
                near_wait(c, way)
                for part in (0, 1):
                    branch = own[part] + near_recv[c, way, part].astype(jnp.float32)
                    kept = residual[c, part_rows(part)].astype(jnp.float32)
                    twin_send[c, part_rows(part)] = (kept + branch).astype(jnp.bfloat16)
                twin_copy(c).start()

    def finish_twin(c):
        for way, here in ((DOWN, s < RUN), (UP, s >= RUN)):
            @pl.when(here)
            def _():
                twin_copy(c).wait_recv()
                near_wait(c, way)
                for part in (0, 1):
                    summed = twin_recv[c, part_rows(part)].astype(jnp.float32) + near_recv[c, way, part].astype(jnp.float32)
                    layer[c, part_rows(part)] = summed.astype(jnp.bfloat16)
        hand_copy(c).start()

    def mix(place):
        entry = table[(z + STEPS[place]) % SIDE]
        slot = lax.broadcasted_iota(jnp.int32, (group, rows), 0).astype(jnp.float32) + (z * group).astype(jnp.float32)
        weights = jnp.where(slot == entry[0:1], entry[2:3], 0.0) + jnp.where(slot == entry[1:2], entry[3:4], 0.0)
        mixing[place] = weights.T.astype(jnp.bfloat16)

    def sent(c, *parts):
        for part in parts:
            for step in (1, 2, 3):
                y_copy(c, step, part).wait_send()
        for way in (UP, DOWN):
            far_copy(c, way).wait_send()
            for part in (0, 1):
                near_copy(c, way, part).wait_send()

        @pl.when(last)
        def _():
            twin_copy(c).wait_send()

    load_hidden(0).wait()
    load_weight(0).wait()
    produce_block(0, 0)
    pl.semaphore_wait(barrier, len(partners) + jnp.where(last, 2, 0))
    for step in (1, 2, 3):
        table_copy(step).start()
    y_start(0, FAR)
    for c in range(1, READ):
        load_weight(c).start()
    for place in (1, 2, 3):
        load_hidden(place).wait()
        produce_block(0, place)
        if place == 2:
            y_start(0, NEAR)
    y_start(0, OWN)
    for step in (1, 2, 3):
        table_copy(step).wait_recv()
    mix(0)
    y_wait(0, FAR)
    send_far(0)
    produce(1)
    y_start(1, FAR, NEAR, OWN)
    mix(1)
    mix(2)
    y_wait(0, NEAR)
    send_near(0)
    mix(3)
    load_residual(0).start()
    load_residual(1).start()
    for c in range(2, AHEAD + 2):
        produce(c)
        if c <= AHEAD:
            y_start(c, ALL)
    y_wait(0, OWN)

    def turn(i):
        split = isinstance(i, int)

        @pl.when(i < chunks - AHEAD)
        def _():
            y_start(i + AHEAD, ALL)

        @pl.when(i <= chunks - READ)
        def _():
            load_weight(i + READ - 1).start()

        @pl.when(i < chunks - 1)
        def _():
            load_residual(i + 1).start()

        @pl.when(i < chunks)
        def _():
            y_wait(i, FAR if split else ALL)
            send_far(i)
            if split:
                y_wait(i, NEAR)
            send_near(i)

        @pl.when(i < chunks - AHEAD - 1)
        def _():
            produce(i + AHEAD + 1)

        @pl.when(i <= chunks)
        def _():
            pass_on(i - 1)

        if split:
            y_wait(i, OWN)
            return

        @pl.when(i < chunks + 2)
        def _():
            finish(i - 2)

        @pl.when(last & (i >= 3))
        def _():
            finish_twin(i - 3)

        @pl.when(i >= 6)
        def _():
            sent(i - 4, ALL)

        @pl.when(i >= 8)
        def _():
            hand_copy(i - 8).wait()

    turn(1)
    pl.loop(2, chunks + 3)(turn)

    sent(0, FAR, NEAR, OWN)
    sent(1, FAR, NEAR, OWN)
    sent(chunks - 1, ALL)

    @pl.loop(chunks - 5, chunks)
    def _(c):
        hand_copy(c).wait()

    for step in (1, 2, 3):
        table_copy(step).wait_send()


def local(hidden, down_weight, expert_ids, route_gates, residual):
    sections = lax.axis_size("section")
    slots, depth = hidden.shape[2:]
    rows, width = residual.shape
    cap = slots // (SIDE * SIDE)
    chunks = width // CHUNK
    group = SIDE * cap
    bf16, f32 = jnp.bfloat16, jnp.float32
    anywhere = pl.BlockSpec(memory_space=pl.ANY)
    in_hbm = pl.BlockSpec(memory_space=pltpu.HBM)
    vmem = pl.BlockSpec(memory_space=pltpu.VMEM)
    dma = pltpu.SemaphoreType.DMA
    return pl.pallas_call(
        functools.partial(kernel, sections, chunks, cap),
        out_shape=pltpu.VMEM((rows, width), bf16) if IN_VMEM else jax.ShapeDtypeStruct((rows, width), bf16),
        in_specs=[in_hbm, in_hbm, vmem, vmem, in_hbm],
        out_specs=vmem if IN_VMEM else anywhere,
        scratch_shapes=[
            pltpu.VMEM((SIDE, group, depth), bf16),
            pltpu.VMEM((chunks, depth, CHUNK), bf16),
            pltpu.VMEM((chunks, rows, CHUNK), bf16),
            pltpu.VMEM((chunks, SIDE, SIDE, cap, CHUNK), bf16),
            pltpu.VMEM((chunks, SIDE, SIDE, cap, CHUNK), bf16),
            pltpu.VMEM((chunks, 2, rows // 2, CHUNK), bf16),
            pltpu.VMEM((chunks, 2, rows // 2, CHUNK), bf16),
            pltpu.VMEM((chunks, 2, 2, rows // 2, CHUNK), bf16),
            pltpu.VMEM((chunks, 2, 2, rows // 2, CHUNK), bf16),
            pltpu.VMEM((chunks, rows, CHUNK), bf16),
            pltpu.VMEM((chunks, rows, CHUNK), bf16),
            pltpu.VMEM((chunks, rows, CHUNK), bf16),
            pltpu.VMEM((SIDE, 8, rows), f32),
            pltpu.VMEM((SIDE, rows, group), bf16),
            dma((SIDE,)), dma((chunks,)), dma((chunks,)), dma((3,)), dma((3,)),
            dma((chunks, 3, 3)), dma((chunks, 3, 3)),
            dma((chunks, 2)), dma((chunks, 2)),
            dma((chunks, 2, 2)), dma((chunks, 2, 2)),
            dma((chunks,)), dma((chunks,)),
            dma((chunks,)), dma((chunks,)),
        ],
        compiler_params=pltpu.CompilerParams(
            collective_id=0, has_side_effects=True, vmem_limit_bytes=(61 if IN_VMEM else 56) * 2**20
        ),
        cost_estimate=pl.CostEstimate(
            flops=2 * slots * width * (depth + rows), bytes_accessed=2 * (slots * depth + depth * width + 2 * rows * width),
            transcendentals=0,
        ),
        name="down_combine_handoff",
    )(hidden, down_weight, expert_ids.T, route_gates.T, residual)


def solution(mesh):
    return jax.shard_map(
        local,
        mesh=mesh,
        in_specs=(
            P("section", "expert", None, None),
            P("section", "expert", None, None),
            P(("section", "expert"), None),
            P(("section", "expert"), None),
            P(("section", "expert"), None),
        ),
        out_specs=P(("section", "expert"), None),
        check_vma=False,
    )
```

time: 165 us -> 148 us (0.90)
  the two profiles are of different devices: /device:TPU:32 before, /device:TPU:1 now
where the time goes in v2:
time: 148 us
  Pallas kernels  147 us (99%)
    pallas_call x1, Pallas kernels, local(): pl.pallas_call(functools.partial(kernel, sections, chunks, cap), out_shap...  147 us

profile of v2, /device:TPU:1, one launch (start us, length us, event | category | flops | bytes accessed | tf_op | source)
XLA Modules:
  0.0 148.2 jit_solution(7282374708498318167)
XLA Ops:
  0.0 147.0 %down_combine_handoff.1 = bf16[256,3584]{1,0:T(8,128)(2,1)S(1)} custom-call(bf16[1,1,1024,1024]{3,2,1,0:T(8,128)(2,1)} %hidden_hbm.1, bf16[1,1,1024,3584]{3,2,1,0:T(8,128)(2,1)} %weight_hbm.1, s32[2,256]{1,0:T(2,128)} %bitcast.2, bf16[2,256]{1,0:T(2,128)(2,1)} %bitcast.3, bf16[256,3584]{1,0:T(8,128)(2,1)} %residual_hbm.1), custom_call_target="tpu_custom_call" | custom-call | flops 9395240960 | bytes 13107200 | tf_op jit(solution)/shard_map/down_combine_handoff/pallas_call | solution.py:359
  147.0 1.2 copy.7

commit v3 on v2

--- a/solution.py
+++ b/solution.py
@@ -11,8 +11,8 @@
 SIDE = 4
 RUN = 8
 CHUNK = 256
-IN_VMEM = True
-READ = 4
+READ = 5
+SPLIT = 2
 AHEAD = 1
 STEPS = (2, 1, 3, 0)
 FAR, NEAR, OWN = slice(0, 1), slice(1, 3), slice(3, 4)
@@ -23,11 +23,11 @@
 def kernel(
     sections, chunks, cap,
     hidden_hbm, weight_hbm, ids_ref, gates_ref, residual_hbm,
-    out_hbm,
+    out_ref,
     hidden, weight, residual, ysend, yrecv, far_send, far_recv, near_send, near_recv, twin_send, twin_recv, layer,
     table, mixing,
     hidden_sem, weight_sem, residual_sem, table_send, table_recv,
-    y_ssem, y_rsem, far_ssem, far_rsem, near_ssem, near_rsem, twin_ssem, twin_rsem, hand_ssem, hand_rsem,
+    y_ssem, first_rsem, y_rsem, far_ssem, far_rsem, near_ssem, near_rsem, twin_ssem, twin_rsem, hand_ssem, hand_rsem,
 ):
     s, e = lax.axis_index("section"), lax.axis_index("expert")
     z, y = e // SIDE, e % SIDE
@@ -64,8 +64,10 @@
     def load_weight(c):
         return pltpu.make_async_copy(weight_hbm.at[0, 0, :, columns(c)], weight.at[c], weight_sem.at[c])
 
-    def load_residual(c):
-        return pltpu.make_async_copy(residual_hbm.at[:, columns(c)], residual.at[c], residual_sem.at[c])
+    load_residual = pltpu.make_async_copy(residual_hbm, residual, residual_sem)
+
+    def drain(ref, sem):
+        pltpu.make_async_copy(ref, ref, sem).wait()
 
     def load_hidden(place):
         block = pl.ds(pl.multiple_of(((z + STEPS[place]) % SIDE) * group, group), group)
@@ -101,10 +103,10 @@
 
     def y_copy(c, step, part):
         yd = (y + step) % SIDE
-        number = (FAR, NEAR, OWN, ALL).index(part) % 3
+        arrival = y_rsem.at[c] if part == ALL else first_rsem.at[c, (FAR, NEAR, OWN).index(part)]
         return pltpu.make_async_remote_copy(
             src_ref=ysend.at[c, yd, part], dst_ref=yrecv.at[c, part, y],
-            send_sem=y_ssem.at[c, step - 1, number], recv_sem=y_rsem.at[c, step - 1, number],
+            send_sem=y_ssem, recv_sem=arrival,
             device_id=at_y(step), device_id_type=MESH,
         )
 
@@ -114,20 +116,20 @@
                 y_copy(c, step, part).start()
 
     def y_wait(c, part):
-        for step in (1, 2, 3):
-            y_copy(c, step, part).wait_recv()
+        arrival = y_rsem.at[c] if part == ALL else first_rsem.at[c, (FAR, NEAR, OWN).index(part)]
+        drain(yrecv.at[c, part, slice(0, 3)], arrival)
 
     def table_copy(step):
         return pltpu.make_async_remote_copy(
             src_ref=table.at[z], dst_ref=table.at[z],
-            send_sem=table_send.at[step - 1], recv_sem=table_recv.at[step - 1],
+            send_sem=table_send, recv_sem=table_recv,
             device_id=at_z(step), device_id_type=MESH,
         )
 
     def far_copy(c, way):
         return pltpu.make_async_remote_copy(
             src_ref=far_send.at[c, way], dst_ref=far_recv.at[c, way],
-            send_sem=far_ssem.at[c, way], recv_sem=far_rsem.at[c, way],
+            send_sem=far_ssem, recv_sem=far_rsem.at[c],
             device_id=at_z(1 if way == UP else 3), device_id_type=MESH,
         )
 
@@ -136,29 +138,24 @@
         slot = jnp.where(lend, 1 - way, way)
         return pltpu.make_async_remote_copy(
             src_ref=near_send.at[c, way, part], dst_ref=near_recv.at[c, slot, part],
-            send_sem=near_ssem.at[c, way, part], recv_sem=near_rsem.at[c, slot, part],
+            send_sem=near_ssem, recv_sem=near_rsem.at[c, slot],
             device_id=at_z(1 if way == UP else 3, jnp.where(lend, twin, s)), device_id_type=MESH,
         )
 
     def near_wait(c, way):
-        for part in (0, 1):
-            pltpu.make_async_remote_copy(
-                src_ref=near_send.at[c, way, part], dst_ref=near_recv.at[c, way, part],
-                send_sem=near_ssem.at[c, way, part], recv_sem=near_rsem.at[c, way, part],
-                device_id=at_z(1), device_id_type=MESH,
-            ).wait_recv()
+        drain(near_recv.at[c, way], near_rsem.at[c, way])
 
     def twin_copy(c):
         return pltpu.make_async_remote_copy(
             src_ref=twin_send.at[c], dst_ref=twin_recv.at[c],
-            send_sem=twin_ssem.at[c], recv_sem=twin_rsem.at[c],
+            send_sem=twin_ssem, recv_sem=twin_rsem.at[c],
             device_id=(twin, e), device_id_type=MESH,
         )
 
     def hand_copy(c):
         return pltpu.make_async_remote_copy(
-            src_ref=layer.at[c], dst_ref=out_hbm.at[:, columns(c)],
-            send_sem=hand_ssem.at[c], recv_sem=hand_rsem.at[c],
+            src_ref=layer.at[c], dst_ref=out_ref.at[:, columns(c)],
+            send_sem=hand_ssem, recv_sem=hand_rsem,
             device_id=following, device_id_type=MESH,
         )
 
@@ -181,14 +178,13 @@
             near_copy(c, way, way).start()
 
     def pass_on(c):
+        own = [partial(c, 1 if way == UP else 3, 1 - way) for way in (UP, DOWN)]
+        drain(far_recv.at[c], far_rsem.at[c])
         for way in (UP, DOWN):
-            own = partial(c, 1 if way == UP else 3, 1 - way)
-            far_copy(c, way).wait_recv()
-            near_send[c, way, 1 - way] = (own + far_recv[c, way].astype(jnp.float32)).astype(jnp.bfloat16)
+            near_send[c, way, 1 - way] = (own[way] + far_recv[c, way].astype(jnp.float32)).astype(jnp.bfloat16)
             near_copy(c, way, 1 - way).start()
 
     def finish(c):
-        load_residual(c).wait()
 
         @pl.when(jnp.logical_not(last))
         def _():
@@ -198,7 +194,7 @@
             for part in (0, 1):
                 branch = own[part] + near_recv[c, UP, part].astype(jnp.float32) + near_recv[c, DOWN, part].astype(jnp.float32)
                 branch = branch.astype(jnp.bfloat16).astype(jnp.float32)
-                kept = residual[c, part_rows(part)].astype(jnp.float32)
+                kept = residual[part_rows(part), columns(c)].astype(jnp.float32)
                 layer[c, part_rows(part)] = (kept + branch).astype(jnp.bfloat16)
             hand_copy(c).start()
 
@@ -209,7 +205,7 @@
                 near_wait(c, way)
                 for part in (0, 1):
                     branch = own[part] + near_recv[c, way, part].astype(jnp.float32)
-                    kept = residual[c, part_rows(part)].astype(jnp.float32)
+                    kept = residual[part_rows(part), columns(c)].astype(jnp.float32)
                     twin_send[c, part_rows(part)] = (kept + branch).astype(jnp.bfloat16)
                 twin_copy(c).start()
 
@@ -229,19 +225,6 @@
         slot = lax.broadcasted_iota(jnp.int32, (group, rows), 0).astype(jnp.float32) + (z * group).astype(jnp.float32)
         weights = jnp.where(slot == entry[0:1], entry[2:3], 0.0) + jnp.where(slot == entry[1:2], entry[3:4], 0.0)
         mixing[place] = weights.T.astype(jnp.bfloat16)
-
-    def sent(c, *parts):
-        for part in parts:
-            for step in (1, 2, 3):
-                y_copy(c, step, part).wait_send()
-        for way in (UP, DOWN):
-            far_copy(c, way).wait_send()
-            for part in (0, 1):
-                near_copy(c, way, part).wait_send()
-
-        @pl.when(last)
-        def _():
-            twin_copy(c).wait_send()
 
     load_hidden(0).wait()
     load_weight(0).wait()
@@ -258,90 +241,77 @@
         if place == 2:
             y_start(0, NEAR)
     y_start(0, OWN)
-    for step in (1, 2, 3):
-        table_copy(step).wait_recv()
+    drain(table.at[0:3], table_recv)
+    def parts(c):
+        return (FAR, NEAR, OWN) if isinstance(c, int) and c < SPLIT else (ALL,)
+
     mix(0)
     y_wait(0, FAR)
     send_far(0)
     produce(1)
-    y_start(1, FAR, NEAR, OWN)
-    mix(1)
-    mix(2)
-    y_wait(0, NEAR)
-    send_near(0)
-    mix(3)
-    load_residual(0).start()
-    load_residual(1).start()
+    y_start(1, *parts(1))
+    for place in (1, 2, 3):
+        mix(place)
+    load_residual.start()
+
+    def turn(i):
+        @pl.when(i < chunks - AHEAD - 1)
+        def _():
+            y_start(i + AHEAD + 1, *parts(i + AHEAD + 1))
+
+        @pl.when(i < chunks - READ)
+        def _():
+            load_weight(i + READ).start()
+
+        @pl.when(i < chunks)
+        def _():
+            for part in parts(i)[1:]:
+                y_wait(i, part)
+            send_near(i)
+
+        @pl.when((i >= 1) & (i <= chunks))
+        def _():
+            pass_on(i - 1)
+
+        @pl.when(i < chunks - 1)
+        def _():
+            y_wait(i + 1, parts(i + 1)[0])
+            send_far(i + 1)
+
+        @pl.when(i < chunks - AHEAD - 2)
+        def _():
+            produce(i + AHEAD + 2)
+
+        @pl.when((i >= 2) & (i < chunks + 2))
+        def _():
+            finish(i - 2)
+
+        @pl.when(last & (i >= 3))
+        def _():
+            finish_twin(i - 3)
+
     for c in range(2, AHEAD + 2):
         produce(c)
         if c <= AHEAD:
-            y_start(c, ALL)
-    y_wait(0, OWN)
-
-    def turn(i):
-        split = isinstance(i, int)
-
-        @pl.when(i < chunks - AHEAD)
-        def _():
-            y_start(i + AHEAD, ALL)
-
-        @pl.when(i <= chunks - READ)
-        def _():
-            load_weight(i + READ - 1).start()
-
-        @pl.when(i < chunks - 1)
-        def _():
-            load_residual(i + 1).start()
-
-        @pl.when(i < chunks)
-        def _():
-            y_wait(i, FAR if split else ALL)
-            send_far(i)
-            if split:
-                y_wait(i, NEAR)
-            send_near(i)
-
-        @pl.when(i < chunks - AHEAD - 1)
-        def _():
-            produce(i + AHEAD + 1)
-
-        @pl.when(i <= chunks)
-        def _():
-            pass_on(i - 1)
-
-        if split:
-            y_wait(i, OWN)
-            return
-
-        @pl.when(i < chunks + 2)
-        def _():
-            finish(i - 2)
-
-        @pl.when(last & (i >= 3))
-        def _():
-            finish_twin(i - 3)
-
-        @pl.when(i >= 6)
-        def _():
-            sent(i - 4, ALL)
-
-        @pl.when(i >= 8)
-        def _():
-            hand_copy(i - 8).wait()
-
-    turn(1)
-    pl.loop(2, chunks + 3)(turn)
-
-    sent(0, FAR, NEAR, OWN)
-    sent(1, FAR, NEAR, OWN)
-    sent(chunks - 1, ALL)
-
-    @pl.loop(chunks - 5, chunks)
-    def _(c):
-        hand_copy(c).wait()
-
-    for step in (1, 2, 3):
-        table_copy(step).wait_send()
+            y_start(c, *parts(c))
+    for i in range(2):
+        turn(i)
+    load_residual.wait()
+    for i in range(2, SPLIT):
+        turn(i)
+    pl.loop(SPLIT, chunks + 3)(turn)
+
+    drain(table.at[0:3], table_send)
+    drain(ysend.at[:, 0:3], y_ssem)
+    drain(far_send, far_ssem)
+    drain(near_send, near_ssem)
+
+    @pl.when(last)
+    def _():
+        drain(twin_send, twin_ssem)
+
+    drain(layer, hand_ssem)
+    drain(layer, hand_rsem)
 
 
 def local(hidden, down_weight, expert_ids, route_gates, residual):
@@ -352,19 +322,18 @@
     chunks = width // CHUNK
     group = SIDE * cap
     bf16, f32 = jnp.bfloat16, jnp.float32
-    anywhere = pl.BlockSpec(memory_space=pl.ANY)
     in_hbm = pl.BlockSpec(memory_space=pltpu.HBM)
     vmem = pl.BlockSpec(memory_space=pltpu.VMEM)
     dma = pltpu.SemaphoreType.DMA
     return pl.pallas_call(
         functools.partial(kernel, sections, chunks, cap),
-        out_shape=pltpu.VMEM((rows, width), bf16) if IN_VMEM else jax.ShapeDtypeStruct((rows, width), bf16),
+        out_shape=pltpu.VMEM((rows, width), bf16),
         in_specs=[in_hbm, in_hbm, vmem, vmem, in_hbm],
-        out_specs=vmem if IN_VMEM else anywhere,
+        out_specs=vmem,
         scratch_shapes=[
             pltpu.VMEM((SIDE, group, depth), bf16),
             pltpu.VMEM((chunks, depth, CHUNK), bf16),
-            pltpu.VMEM((chunks, rows, CHUNK), bf16),
+            pltpu.VMEM((rows, width), bf16),
             pltpu.VMEM((chunks, SIDE, SIDE, cap, CHUNK), bf16),
             pltpu.VMEM((chunks, SIDE, SIDE, cap, CHUNK), bf16),
             pltpu.VMEM((chunks, 2, rows // 2, CHUNK), bf16),
@@ -376,15 +345,15 @@
             pltpu.VMEM((chunks, rows, CHUNK), bf16),
             pltpu.VMEM((SIDE, 8, rows), f32),
             pltpu.VMEM((SIDE, rows, group), bf16),
-            dma((SIDE,)), dma((chunks,)), dma((chunks,)), dma((3,)), dma((3,)),
-            dma((chunks, 3, 3)), dma((chunks, 3, 3)),
-            dma((chunks, 2)), dma((chunks, 2)),
-            dma((chunks, 2, 2)), dma((chunks, 2, 2)),
-            dma((chunks,)), dma((chunks,)),
-            dma((chunks,)), dma((chunks,)),
+            dma((SIDE,)), dma((chunks,)), dma(()), dma(()), dma(()),
+            dma(()), dma((SPLIT, 3)), dma((chunks,)),
+            dma(()), dma((chunks,)),
+            dma(()), dma((chunks, 2)),
+            dma(()), dma((chunks,)),
+            dma(()), dma(()),
         ],
         compiler_params=pltpu.CompilerParams(
-            collective_id=0, has_side_effects=True, vmem_limit_bytes=(61 if IN_VMEM else 56) * 2**20
+            collective_id=0, has_side_effects=True, vmem_limit_bytes=61 * 2**20
         ),
         cost_estimate=pl.CostEstimate(
             flops=2 * slots * width * (depth + rows), bytes_accessed=2 * (slots * depth + depth * width + 2 * rows * width),

time: 148 us -> 143 us (0.966)
  the two profiles are of different devices: /device:TPU:1 before, /device:TPU:32 now
where the time goes in v3:
time: 143 us
  Pallas kernels  142 us (99%)
    pallas_call x1, Pallas kernels, local(): pl.pallas_call(functools.partial(kernel, sections, chunks, cap), out_shap...  142 us

profile of v3, /device:TPU:32, one launch (start us, length us, event | category | flops | bytes accessed | tf_op | source)
XLA Modules:
  0.0 142.9 jit_solution(7999800051423793449)
XLA Ops:
  0.0 141.7 %down_combine_handoff.1 = bf16[256,3584]{1,0:T(8,128)(2,1)S(1)} custom-call(bf16[1,1,1024,1024]{3,2,1,0:T(8,128)(2,1)} %hidden_hbm.1, bf16[1,1,1024,3584]{3,2,1,0:T(8,128)(2,1)} %weight_hbm.1, s32[2,256]{1,0:T(2,128)} %bitcast.2, bf16[2,256]{1,0:T(2,128)(2,1)} %bitcast.3, bf16[256,3584]{1,0:T(8,128)(2,1)} %residual_hbm.1), custom_call_target="tpu_custom_call" | custom-call | flops 9395240960 | bytes 13107200 | tf_op jit(solution)/shard_map/down_combine_handoff/pallas_call | solution.py:328
  141.7 1.2 copy.7

commit v4 on v3

--- a/solution.py
+++ b/solution.py
@@ -17,6 +17,7 @@
 STEPS = (2, 1, 3, 0)
 FAR, NEAR, OWN = slice(0, 1), slice(1, 3), slice(3, 4)
 ALL = slice(0, 4)
+LAG = 2
 UP, DOWN = 0, 1
 
 
@@ -152,15 +153,15 @@
             device_id=(twin, e), device_id_type=MESH,
         )
 
-    def hand_copy(c):
-        return pltpu.make_async_remote_copy(
-            src_ref=layer.at[c], dst_ref=out_ref.at[:, columns(c)],
+    def part_rows(part):
+        return slice(part * half, (part + 1) * half)
+
+    def hand_copy(c, part):
+        return pltpu.make_async_remote_copy(
+            src_ref=layer.at[c, part_rows(part)], dst_ref=out_ref.at[part_rows(part), columns(c)],
             send_sem=hand_ssem, recv_sem=hand_rsem,
             device_id=following, device_id_type=MESH,
         )
-
-    def part_rows(part):
-        return slice(part * half, (part + 1) * half)
 
     def partial(c, step, part):
         place = STEPS.index(step)
@@ -196,7 +197,7 @@
                 branch = branch.astype(jnp.bfloat16).astype(jnp.float32)
                 kept = residual[part_rows(part), columns(c)].astype(jnp.float32)
                 layer[c, part_rows(part)] = (kept + branch).astype(jnp.bfloat16)
-            hand_copy(c).start()
+                hand_copy(c, part).start()
 
         for way, here in ((UP, s < RUN), (DOWN, s >= RUN)):
             @pl.when(last & here)
@@ -218,7 +219,7 @@
                 for part in (0, 1):
                     summed = twin_recv[c, part_rows(part)].astype(jnp.float32) + near_recv[c, way, part].astype(jnp.float32)
                     layer[c, part_rows(part)] = summed.astype(jnp.bfloat16)
-        hand_copy(c).start()
+                    hand_copy(c, part).start()
 
     def mix(place):
         entry = table[(z + STEPS[place]) % SIDE]
@@ -282,13 +283,13 @@
         def _():
             produce(i + AHEAD + 2)
 
-        @pl.when((i >= 2) & (i < chunks + 2))
-        def _():
-            finish(i - 2)
-
-        @pl.when(last & (i >= 3))
-        def _():
-            finish_twin(i - 3)
+        @pl.when((i >= LAG) & (i < chunks + LAG))
+        def _():
+            finish(i - LAG)
+
+        @pl.when(last & (i > LAG))
+        def _():
+            finish_twin(i - LAG - 1)
 
     for c in range(2, AHEAD + 2):
         produce(c)
@@ -299,7 +300,7 @@
     load_residual.wait()
     for i in range(2, SPLIT):
         turn(i)
-    pl.loop(SPLIT, chunks + 3)(turn)
+    pl.loop(SPLIT, chunks + LAG + 1)(turn)
 
     drain(table.at[0:3], table_send)
     drain(ysend.at[:, 0:3], y_ssem)

time: 143 us -> 143 us (level)
  no operation moved by 1% of the time
where the time goes in v4:
time: 143 us
  Pallas kernels  142 us (99%)
    pallas_call x1, Pallas kernels, local(): pl.pallas_call(functools.partial(kernel, sections, chunks, cap), out_shap...  142 us

profile of v4, /device:TPU:32, one launch (start us, length us, event | category | flops | bytes accessed | tf_op | source)
XLA Modules:
  0.0 142.9 jit_solution(18142036052749676534)
XLA Ops:
  0.0 141.7 %down_combine_handoff.1 = bf16[256,3584]{1,0:T(8,128)(2,1)S(1)} custom-call(bf16[1,1,1024,1024]{3,2,1,0:T(8,128)(2,1)} %hidden_hbm.1, bf16[1,1,1024,3584]{3,2,1,0:T(8,128)(2,1)} %weight_hbm.1, s32[2,256]{1,0:T(2,128)} %bitcast.2, bf16[2,256]{1,0:T(2,128)(2,1)} %bitcast.3, bf16[256,3584]{1,0:T(8,128)(2,1)} %residual_hbm.1), custom_call_target="tpu_custom_call" | custom-call | flops 9395240960 | bytes 13107200 | tf_op jit(solution)/shard_map/down_combine_handoff/pallas_call | solution.py:329
  141.7 1.2 copy.7

commit v5 on v3

--- a/solution.py
+++ b/solution.py
@@ -17,6 +17,7 @@
 STEPS = (2, 1, 3, 0)
 FAR, NEAR, OWN = slice(0, 1), slice(1, 3), slice(3, 4)
 ALL = slice(0, 4)
+RING = 4
 UP, DOWN = 0, 1
 
 
@@ -62,7 +63,7 @@
         return pl.ds(pl.multiple_of(c * CHUNK, CHUNK), CHUNK)
 
     def load_weight(c):
-        return pltpu.make_async_copy(weight_hbm.at[0, 0, :, columns(c)], weight.at[c], weight_sem.at[c])
+        return pltpu.make_async_copy(weight_hbm.at[0, 0, :, columns(c)], weight.at[c], weight_sem.at[c % (2 * RING)])
 
     load_residual = pltpu.make_async_copy(residual_hbm, residual, residual_sem)
 
@@ -103,7 +104,7 @@
 
     def y_copy(c, step, part):
         yd = (y + step) % SIDE
-        arrival = y_rsem.at[c] if part == ALL else first_rsem.at[c, (FAR, NEAR, OWN).index(part)]
+        arrival = y_rsem.at[c % RING] if part == ALL else first_rsem.at[c, (FAR, NEAR, OWN).index(part)]
         return pltpu.make_async_remote_copy(
             src_ref=ysend.at[c, yd, part], dst_ref=yrecv.at[c, part, y],
             send_sem=y_ssem, recv_sem=arrival,
@@ -116,7 +117,7 @@
                 y_copy(c, step, part).start()
 
     def y_wait(c, part):
-        arrival = y_rsem.at[c] if part == ALL else first_rsem.at[c, (FAR, NEAR, OWN).index(part)]
+        arrival = y_rsem.at[c % RING] if part == ALL else first_rsem.at[c, (FAR, NEAR, OWN).index(part)]
         drain(yrecv.at[c, part, slice(0, 3)], arrival)
 
     def table_copy(step):
@@ -129,7 +130,7 @@
     def far_copy(c, way):
         return pltpu.make_async_remote_copy(
             src_ref=far_send.at[c, way], dst_ref=far_recv.at[c, way],
-            send_sem=far_ssem, recv_sem=far_rsem.at[c],
+            send_sem=far_ssem, recv_sem=far_rsem.at[c % RING],
             device_id=at_z(1 if way == UP else 3), device_id_type=MESH,
         )
 
@@ -138,17 +139,17 @@
         slot = jnp.where(lend, 1 - way, way)
         return pltpu.make_async_remote_copy(
             src_ref=near_send.at[c, way, part], dst_ref=near_recv.at[c, slot, part],
-            send_sem=near_ssem, recv_sem=near_rsem.at[c, slot],
+            send_sem=near_ssem, recv_sem=near_rsem.at[c % (2 * RING), slot],
             device_id=at_z(1 if way == UP else 3, jnp.where(lend, twin, s)), device_id_type=MESH,
         )
 
     def near_wait(c, way):
-        drain(near_recv.at[c, way], near_rsem.at[c, way])
+        drain(near_recv.at[c, way], near_rsem.at[c % (2 * RING), way])
 
     def twin_copy(c):
         return pltpu.make_async_remote_copy(
             src_ref=twin_send.at[c], dst_ref=twin_recv.at[c],
-            send_sem=twin_ssem, recv_sem=twin_rsem.at[c],
+            send_sem=twin_ssem, recv_sem=twin_rsem.at[c % RING],
             device_id=(twin, e), device_id_type=MESH,
         )
 
@@ -179,7 +180,7 @@
 
     def pass_on(c):
         own = [partial(c, 1 if way == UP else 3, 1 - way) for way in (UP, DOWN)]
-        drain(far_recv.at[c], far_rsem.at[c])
+        drain(far_recv.at[c], far_rsem.at[c % RING])
         for way in (UP, DOWN):
             near_send[c, way, 1 - way] = (own[way] + far_recv[c, way].astype(jnp.float32)).astype(jnp.bfloat16)
             near_copy(c, way, 1 - way).start()
@@ -345,11 +346,11 @@
             pltpu.VMEM((chunks, rows, CHUNK), bf16),
             pltpu.VMEM((SIDE, 8, rows), f32),
             pltpu.VMEM((SIDE, rows, group), bf16),
-            dma((SIDE,)), dma((chunks,)), dma(()), dma(()), dma(()),
-            dma(()), dma((SPLIT, 3)), dma((chunks,)),
-            dma(()), dma((chunks,)),
-            dma(()), dma((chunks, 2)),
-            dma(()), dma((chunks,)),
+            dma((SIDE,)), dma((2 * RING,)), dma(()), dma(()), dma(()),
+            dma(()), dma((SPLIT, 3)), dma((RING,)),
+            dma(()), dma((RING,)),
+            dma(()), dma((2 * RING, 2)),
+            dma(()), dma((RING,)),
             dma(()), dma(()),
         ],
         compiler_params=pltpu.CompilerParams(

time: 143 us -> 143 us (level)
  no operation moved by 1% of the time
where the time goes in v5:
time: 143 us
  Pallas kernels  141 us (99%)
    pallas_call x1, Pallas kernels, local(): pl.pallas_call(functools.partial(kernel, sections, chunks, cap), out_shap...  141 us

profile of v5, /device:TPU:32, one launch (start us, length us, event | category | flops | bytes accessed | tf_op | source)
XLA Modules:
  0.0 142.6 jit_solution(7638032787630917901)
XLA Ops:
  0.0 141.3 %down_combine_handoff.1 = bf16[256,3584]{1,0:T(8,128)(2,1)S(1)} custom-call(bf16[1,1,1024,1024]{3,2,1,0:T(8,128)(2,1)} %hidden_hbm.1, bf16[1,1,1024,3584]{3,2,1,0:T(8,128)(2,1)} %weight_hbm.1, s32[2,256]{1,0:T(2,128)} %bitcast.2, bf16[2,256]{1,0:T(2,128)(2,1)} %bitcast.3, bf16[256,3584]{1,0:T(8,128)(2,1)} %residual_hbm.1), custom_call_target="tpu_custom_call" | custom-call | flops 9395240960 | bytes 13107200 | tf_op jit(solution)/shard_map/down_combine_handoff/pallas_call | solution.py:329
  141.3 1.2 copy.7
